TPU v7x, 32 devices: a whole 2x2x4 slice. The times are simulated.
32 devices in a mesh: groups: 2 (over y), ctx: 4 (over z), chan: 4 (over x, core).
Axes of the slice: x: 2, y: 2, z: 4, core: 2. Of those that a mesh axis runs over, the one named last changes fastest.
Arguments:
- query_stream: bfloat16 [4096, 2048], P('chan', ('groups', 'ctx')), parts along dimension 1, may hold values from -6 to 6
- key_stream: bfloat16 [4096, 2048], P('chan', ('groups', 'ctx')), parts along dimension 1, may hold values from -6 to 6
- value_stream: bfloat16 [4096, 2048], P('chan', ('groups', 'ctx')), parts along dimension 1, may hold values from -6 to 6
- cotangent: bfloat16 [4096, 2048], P('chan', ('groups', 'ctx')), parts along dimension 1, may hold values from -6 to 6
- filters: float32 [256, 1024], P(None, 'ctx'), may hold values from -1.5 to 1.5
Outputs:
- query_grad: bfloat16 [4096, 2048], P('chan', ('groups', 'ctx')), parts along dimension 1
- key_grad: bfloat16 [4096, 2048], P('chan', ('groups', 'ctx')), parts along dimension 1
- value_grad: bfloat16 [4096, 2048], P('chan', ('groups', 'ctx')), parts along dimension 1
- filter_grad: float32 [256, 2048], P(None, ('groups', 'ctx')), parts along dimension 1
There are 2 independent parts, one for each index of `groups`. A program takes and returns all parts, laid end to end along the dimension named above; an argument that names none is the same for every part. Nothing has to cross between parts.
All inputs are finite; a program needn't handle non-finite values.
Results may differ from a plain program's by a relative error of at most 0.001.
Values may be sent and summed in bfloat16 or wider, within the bound.
A program may use at most 64 MiB of HBM per device.

v0:
```python
import functools
import math

import jax
import jax.numpy as jnp
import numpy as np
from jax import lax
from jax.experimental import pallas as pl
from jax.experimental.pallas import tpu as pltpu
from jax.sharding import PartitionSpec as P

GROUP = 16
MESH = pl.DeviceIdType.MESH
ROWS = 16


def half_tables(block):
    span = np.arange(block, dtype=np.int64)
    turned = ((2 * span[None, :] + 1) * span[:, None]) % (4 * block)
    angle = turned.astype(np.float64) * (math.pi / (2 * block))
    ahead = np.concatenate([np.cos(angle), -np.sin(angle)], axis=1).astype(np.float32)
    back = (np.concatenate([np.cos(angle).T, -np.sin(angle).T], axis=0) / block).astype(np.float32)

    def parts(table):
        high = table.astype(jnp.bfloat16)
        low = (table - high.astype(np.float32)).astype(jnp.bfloat16)
        return high, low

    ahead_high, ahead_low = parts(ahead)
    back_high, back_low = parts(back)
    return (
        np.concatenate([ahead_high, ahead_high, ahead_low], axis=0),
        np.concatenate([back_high, back_high, back_low], axis=0),
    )


def ctx_kernel(
    nchan,
    q_ref,
    k_ref,
    v_ref,
    c_ref,
    filt_ref,
    ahead_ref,
    back_ref,
    qg_ref,
    kg_ref,
    vg_ref,
    fg_ref,
    pair_p,
    pair_a,
    landed,
    filt_all,
    gains,
    spec,
    prep,
    corr,
    agg_out,
    agg_in,
    send_sem,
    recv_sem,
    filt_send,
    filt_recv,
    spread_send,
    spread_recv,
    agg_send,
    agg_recv,
):
    local_ch, block = q_ref.shape
    fcount = filt_ref.shape[0]
    chunks = local_ch // fcount
    quarter = fcount // nchan
    me = lax.axis_index("ctx")
    mine = lax.axis_index("chan")
    f32, bf16 = jnp.float32, jnp.bfloat16

    barrier = pltpu.get_barrier_semaphore()
    for step in range(1, 4):
        pl.semaphore_signal(
            barrier, inc=1, device_id={"ctx": lax.rem(me + step, 4)}, device_id_type=MESH
        )
    for step in range(1, nchan):
        pl.semaphore_signal(
            barrier, inc=1, device_id={"chan": lax.rem(mine + step, nchan)}, device_id_type=MESH
        )

    def split_into(dest, rows, left, right):
        val = left.astype(f32) * right.astype(f32)
        high = val.astype(bf16)
        dest[rows, 0:block] = high
        dest[rows, block : 2 * block] = (val - high.astype(f32)).astype(bf16)

    @pl.loop(0, local_ch // 64)
    def _(i):
        rows = pl.ds(pl.multiple_of(i * 64, 64), 64)
        split_into(pair_p, rows, k_ref[rows, :], v_ref[rows, :])
        split_into(pair_a, rows, c_ref[rows, :], q_ref[rows, :])

    pl.semaphore_wait(barrier, 3 + nchan - 1)

    def move(source, chunk, slot, target):
        rows = pl.ds(chunk * fcount, fcount)
        return pltpu.make_async_remote_copy(
            src_ref=source.at[rows, :],
            dst_ref=landed.at[slot, rows, :],
            send_sem=send_sem.at[slot, chunk],
            recv_sem=recv_sem.at[slot, chunk],
            device_id={"ctx": target},
            device_id_type=MESH,
        )

    def filt_move(owner, target):
        rows = pl.ds(pl.multiple_of(mine * quarter, quarter), quarter)
        return pltpu.make_async_remote_copy(
            src_ref=filt_ref.at[rows, :],
            dst_ref=filt_all.at[owner, rows, :],
            send_sem=filt_send.at[target],
            recv_sem=filt_recv.at[owner],
            device_id={"ctx": target},
            device_id_type=MESH,
        )

    def spread(owner, step):
        rows = pl.ds(pl.multiple_of(mine * quarter, quarter), quarter)
        return pltpu.make_async_remote_copy(
            src_ref=filt_all.at[owner, rows, :],
            dst_ref=filt_all.at[owner, rows, :],
            send_sem=spread_send.at[owner, step],
            recv_sem=spread_recv.at[owner, step],
            device_id={"chan": lax.rem(mine + step, nchan)},
            device_id_type=MESH,
        )

    def agg_move(chunk, target):
        rows = pl.ds(chunk * fcount, fcount)
        return pltpu.make_async_remote_copy(
            src_ref=agg_out.at[rows, :],
            dst_ref=agg_in.at[rows, :],
            send_sem=agg_send.at[chunk],
            recv_sem=agg_recv.at[chunk],
            device_id={"ctx": target},
            device_id_type=MESH,
        )

    def ahead(pairs):
        high = pairs[:, 0:block]
        return jnp.dot(pairs, ahead_ref[0 : 2 * block, :], preferred_element_type=f32) + jnp.dot(
            high, ahead_ref[2 * block : 3 * block, :], preferred_element_type=f32
        )

    def inverse_of(which):
        return jnp.dot(
            prep[which, :, :], back_ref[0 : 4 * block, :], preferred_element_type=f32
        ) + jnp.dot(
            prep[which, :, 0 : 2 * block],
            back_ref[4 * block : 6 * block, :],
            preferred_element_type=f32,
        )

    def put_prep(which, rows, re, im):
        for place, val in ((0, re), (block, im)):
            high = val.astype(bf16)
            prep[which, rows, place : place + block] = high
            prep[which, rows, 2 * block + place : 3 * block + place] = (
                val - high.astype(f32)
            ).astype(bf16)

    def sign_of():
        col = lax.broadcasted_iota(jnp.int32, (ROWS, block), 1)
        return (1 - 2 * lax.rem(col, 2)).astype(f32)

    def role(j):
        inner = j in (1, 2)
        lower = j < 2
        own_u = pair_p if lower else pair_a
        sends = []
        targets = {0: (1, 2, 3), 1: (2,), 2: (1,), 3: (2, 1)}[j]
        needs = {0: (), 1: (0, 2, 3), 2: (0, 1, 3), 3: (0,)}[j]
        for target in targets:
            copy = filt_move(j, target)
            copy.start()
            sends.append(copy)
        for chunk in range(chunks):
            if inner:
                moves = [move(own_u, chunk, 1, 3 - j)]
            else:
                moves = [
                    move(own_u, chunk, 2, 2 if lower else 1),
                    move(own_u, chunk, 0, 1 if lower else 2),
                ]
            for copy in moves:
                copy.start()
                sends.append(copy)
        for owner in needs:
            filt_move(owner, j).wait_recv()
            for step in range(1, nchan):
                copy = spread(owner, step)
                copy.start()
                sends.append(copy)
        filt_all[j, :, :] = filt_ref[...]
        for owner in needs:
            for step in range(1, nchan):
                spread(owner, step).wait_recv()
        used = range(4) if inner else (0,)
        for owner in used:
            val = filt_all[owner, :, :]
            high = val.astype(bf16)
            low = (val - high.astype(f32)).astype(bf16)
            spec[owner, :, :] = ahead(jnp.concatenate([high, low], axis=1))

        @pl.loop(0, fcount // ROWS)
        def _(i):
            rows = pl.ds(pl.multiple_of(i * ROWS, ROWS), ROWS)
            sign = sign_of()
            for d in used:
                re, im = spec[d, rows, 0:block], spec[d, rows, block : 2 * block]
                if d:
                    re = re - sign * spec[d - 1, rows, block : 2 * block]
                    im = im + sign * spec[d - 1, rows, 0:block]
                gains[d, rows, 0:block] = re
                gains[d, rows, block : 2 * block] = im
                corr[d, rows, :] = jnp.zeros((ROWS, 2 * block), f32)

        if inner:
            held_p = {1: (0, 1), 2: (0, 1, 2)}[j]
            held_a = {1: (1, 2, 3), 2: (2, 3)}[j]
        else:
            held_p, held_a = (j,), (j,)
        places = {}
        for i in held_p:
            places["p", i] = len(places)
        for i in held_a:
            places["a", i] = len(places)
        slots = {1: {("p", 0): 0, ("a", 2): 1, ("a", 3): 2}, 2: {("a", 3): 0, ("p", 1): 1, ("p", 0): 2}}
        slots = slots.get(j, {})
        pairs_fg = {
            0: ((0, 0),),
            1: ((1, 1), (0, 1), (1, 2), (1, 3)),
            2: ((2, 2), (2, 3), (0, 2), (0, 3)),
            3: ((3, 3),),
        }[j]

        for chunk in range(chunks):
            crow = pl.ds(chunk * fcount, fcount)
            for name, place in places.items():
                if name in slots:
                    move(own_u, chunk, slots[name], j).wait_recv()
                    spec[place, :, :] = ahead(landed[slots[name], crow, :])
                else:
                    spec[place, :, :] = ahead((pair_p if name[0] == "p" else pair_a)[crow, :])

            @pl.loop(0, fcount // ROWS)
            def _(i):
                rows = pl.ds(pl.multiple_of(i * ROWS, ROWS), ROWS)

                def load(name):
                    at = places[name]
                    return spec[at, rows, 0:block], spec[at, rows, block : 2 * block]

                def gain(d):
                    return gains[d, rows, 0:block], gains[d, rows, block : 2 * block]

                def mixed_to(target):
                    re = im = None
                    for src in held_p:
                        if src > target:
                            continue
                        pr, pi = load(("p", src))
                        gr, gi = gain(target - src)
                        r, m = pr * gr - pi * gi, pr * gi + pi * gr
                        re, im = (r, m) if re is None else (re + r, im + m)
                    return re, im

                def back_to(target):
                    re = im = None
                    for src in held_a:
                        if src < target:
                            continue
                        ar, ai = load(("a", src))
                        gr, gi = gain(src - target)
                        r, m = ar * gr + ai * gi, ai * gr - ar * gi
                        re, im = (r, m) if re is None else (re + r, im + m)
                    return re, im

                put_prep(0, rows, *mixed_to(j))
                put_prep(1, rows, *back_to(j))
                if j == 1:
                    put_prep(2, rows, *back_to(0))
                if j == 2:
                    put_prep(2, rows, *mixed_to(3))
                for src, dst in pairs_fg:
                    pr, pi = load(("p", src))
                    ar, ai = load(("a", dst))
                    d = dst - src
                    corr[d, rows, 0:block] += ar * pr + ai * pi
                    corr[d, rows, block : 2 * block] += ai * pr - ar * pi

            if inner:
                agg_out[crow, :] = inverse_of(2)
                copy = agg_move(chunk, 0 if lower else 3)
                copy.start()
                sends.append(copy)
            if j == 3:
                agg_out[crow, :] = inverse_of(0)
            else:
                qg_ref[crow, :] = (c_ref[crow, :].astype(f32) * inverse_of(0)).astype(bf16)
            if j == 0:
                agg_out[crow, :] = inverse_of(1)
            else:
                back = inverse_of(1)
                kg_ref[crow, :] = (back * v_ref[crow, :].astype(f32)).astype(bf16)
                vg_ref[crow, :] = (back * k_ref[crow, :].astype(f32)).astype(bf16)

        scale = 1.0 / math.sqrt(GROUP * block * 4)
        for b in range(4):
            if b not in used:
                fg_ref[b, :, :] = jnp.zeros((fcount, block), f32)
                continue

            @pl.loop(0, fcount // ROWS)
            def _(i):
                rows = pl.ds(pl.multiple_of(i * ROWS, ROWS), ROWS)
                re, im = corr[b, rows, 0:block], corr[b, rows, block : 2 * block]
                if b + 1 in used:
                    sign = sign_of()
                    re = re + sign * corr[b + 1, rows, block : 2 * block]
                    im = im - sign * corr[b + 1, rows, 0:block]
                put_prep(0, rows, re, im)

            fg_ref[b, :, :] = inverse_of(0) * scale

        if not inner:
            for chunk in range(chunks):
                crow = pl.ds(chunk * fcount, fcount)
                agg_move(chunk, j).wait_recv()
                total = agg_out[crow, :] + agg_in[crow, :]
                if j == 3:
                    qg_ref[crow, :] = (c_ref[crow, :].astype(f32) * total).astype(bf16)
                else:
                    kg_ref[crow, :] = (total * v_ref[crow, :].astype(f32)).astype(bf16)
                    vg_ref[crow, :] = (total * k_ref[crow, :].astype(f32)).astype(bf16)
        for copy in sends:
            copy.wait_send()

    for j in range(4):
        pl.when(me == j)(functools.partial(role, j))


def blocked_body(query_stream, key_stream, value_stream, cotangent, filters):
    local_ch, block = query_stream.shape
    fcount = filters.shape[0]
    nchan = lax.axis_size("chan")
    chunks = local_ch // fcount
    ahead, back = half_tables(block)
    ahead = jnp.asarray(ahead)
    back = jnp.asarray(back)
    vmem = pl.BlockSpec(memory_space=pltpu.VMEM)
    stream = jax.ShapeDtypeStruct((local_ch, block), jnp.bfloat16)
    dma = pltpu.SemaphoreType.DMA
    query_grad, key_grad, value_grad, terms = pl.pallas_call(
        functools.partial(ctx_kernel, nchan),
        out_shape=(
            stream,
            stream,
            stream,
            jax.ShapeDtypeStruct((4, fcount, block), jnp.float32),
        ),
        in_specs=[vmem] * 7,
        out_specs=(vmem,) * 4,
        scratch_shapes=[
            pltpu.VMEM((local_ch, 2 * block), jnp.bfloat16),
            pltpu.VMEM((local_ch, 2 * block), jnp.bfloat16),
            pltpu.VMEM((3, local_ch, 2 * block), jnp.bfloat16),
            pltpu.VMEM((4, fcount, block), jnp.float32),
            pltpu.VMEM((4, fcount, 2 * block), jnp.float32),
            pltpu.VMEM((5, fcount, 2 * block), jnp.float32),
            pltpu.VMEM((3, fcount, 4 * block), jnp.bfloat16),
            pltpu.VMEM((4, fcount, 2 * block), jnp.float32),
            pltpu.VMEM((local_ch, block), jnp.float32),
            pltpu.VMEM((local_ch, block), jnp.float32),
            dma((3, chunks)),
            dma((3, chunks)),
            dma((4,)),
            dma((4,)),
            dma((4, nchan)),
            dma((4, nchan)),
            dma((chunks,)),
            dma((chunks,)),
        ],
        compiler_params=pltpu.CompilerParams(
            collective_id=0, has_side_effects=True, vmem_limit_bytes=48 * 1024 * 1024
        ),
        cost_estimate=pl.CostEstimate(flops=8 * 10**9, bytes_accessed=8 * 10**6, transcendentals=0),
    )(query_stream, key_stream, value_stream, cotangent, filters, ahead, back)
    summed = lax.psum_scatter(terms, "ctx", scatter_dimension=0, tiled=True)
    filter_grad = lax.psum(summed.reshape(fcount, block), "chan")
    return (query_grad, key_grad, value_grad, filter_grad)


highest_mode = lax.Precision.HIGHEST


def turn_table(row_count, col_count, modulus):
    row_span = jnp.arange(row_count, dtype=jnp.int32)
    col_span = jnp.arange(col_count, dtype=jnp.int32)
    turned = row_span[:, None] * col_span[None, :] % modulus
    angle_vals = turned.astype(jnp.float32) * (2.0 * math.pi / modulus)
    return (jnp.cos(angle_vals), jnp.sin(angle_vals))


def split_of(length):
    for candidate in range(32, 1, -1):
        if (
            length % candidate == 0
            and length // candidate >= 128
            and (length // candidate % 128 == 0)
        ):
            return candidate
    return 1


def contract_front(table, operand):
    return jnp.einsum("ac,...ab->...cb", table, operand, precision=highest_mode)


def base_transform(re_part, im_part, sign_value):
    length = re_part.shape[-1]
    cos_table, sin_table = turn_table(length, length, length)
    turn_imag = sign_value * sin_table
    summed = jnp.einsum("...t,tk->...k", re_part + im_part, cos_table, precision=highest_mode)
    left_term = jnp.einsum("...t,tk->...k", re_part, turn_imag - cos_table, precision=highest_mode)
    second = jnp.einsum("...t,tk->...k", im_part, cos_table + turn_imag, precision=highest_mode)
    return (summed - second, summed + left_term)


def twist_forward(y_real, y_imag, length, leading):
    radix_size, inner_len = y_real.shape[-2:]
    cos_twist, sin_twist = turn_table(radix_size, inner_len, length)
    tw_real = y_real * cos_twist + y_imag * sin_twist
    tw_imag = y_imag * cos_twist - y_real * sin_twist
    z_real, z_imag = forward(tw_real, tw_imag)
    return (z_real.reshape(leading + (length,)), z_imag.reshape(leading + (length,)))


def forward(re_part, im_part):
    length = re_part.shape[-1]
    leading = re_part.shape[:-1]
    radix_size = split_of(length)
    if radix_size == 1:
        return base_transform(re_part, im_part, -1.0)
    inner_len = length // radix_size
    re_grid = re_part.reshape(leading + (radix_size, inner_len))
    im_grid = im_part.reshape(leading + (radix_size, inner_len))
    cos_table, sin_table = turn_table(radix_size, radix_size, radix_size)
    y_real = contract_front(cos_table, re_grid) + contract_front(sin_table, im_grid)
    y_imag = contract_front(cos_table, im_grid) - contract_front(sin_table, re_grid)
    return twist_forward(y_real, y_imag, length, leading)


def forward_padded(signal):
    half_len = signal.shape[-1]
    length = 2 * half_len
    leading = signal.shape[:-1]
    radix_size = split_of(length)
    inner_len = length // radix_size
    grid = signal.reshape(leading + (radix_size // 2, inner_len))
    cos_table, sin_table = turn_table(radix_size // 2, radix_size, radix_size)
    y_real = contract_front(cos_table, grid)
    y_imag = -contract_front(sin_table, grid)
    return twist_forward(y_real, y_imag, length, leading)


def untwist(z_real, z_imag, length):
    radix_size, inner_len = z_real.shape[-2:]
    cos_twist, sin_twist = turn_table(radix_size, inner_len, length)
    return (z_real * cos_twist - z_imag * sin_twist, z_imag * cos_twist + z_real * sin_twist)


def inverse(re_part, im_part):
    length = re_part.shape[-1]
    leading = re_part.shape[:-1]
    radix_size = split_of(length)
    if radix_size == 1:
        return base_transform(re_part, im_part, 1.0)
    inner_len = length // radix_size
    z_real, z_imag = inverse(
        re_part.reshape(leading + (radix_size, inner_len)),
        im_part.reshape(leading + (radix_size, inner_len)),
    )
    y_real, y_imag = untwist(z_real, z_imag, length)
    cos_table, sin_table = turn_table(radix_size, radix_size, radix_size)
    x_real = contract_front(cos_table, y_real) - contract_front(sin_table, y_imag)
    x_imag = contract_front(cos_table, y_imag) + contract_front(sin_table, y_real)
    return (x_real.reshape(leading + (length,)), x_imag.reshape(leading + (length,)))


def inverse_half(re_part, im_part):
    length = re_part.shape[-1]
    leading = re_part.shape[:-1]
    radix_size = split_of(length)
    inner_len = length // radix_size
    z_real, z_imag = inverse(
        re_part.reshape(leading + (radix_size, inner_len)),
        im_part.reshape(leading + (radix_size, inner_len)),
    )
    y_real, y_imag = untwist(z_real, z_imag, length)
    cos_table, sin_table = turn_table(radix_size, radix_size // 2, radix_size)
    x_real = contract_front(cos_table, y_real) - contract_front(sin_table, y_imag)
    x_imag = contract_front(cos_table, y_imag) + contract_front(sin_table, y_real)
    return (x_real.reshape(leading + (length // 2,)), x_imag.reshape(leading + (length // 2,)))


def body(query_stream, key_stream, value_stream, cotangent, filters):
    local_ch, length = query_stream.shape
    filter_count = filters.shape[0]
    ctx_count = lax.axis_size("ctx")
    per_device = local_ch // ctx_count
    seq_len = length * ctx_count
    padded_len = 2 * seq_len
    streams = jnp.stack([query_stream, key_stream, value_stream, cotangent], axis=0)
    arrived = lax.all_to_all(streams, "ctx", split_axis=1, concat_axis=2, tiled=True)
    queries = arrived[0].astype(jnp.float32)
    key_data = arrived[1].astype(jnp.float32)
    value_data = arrived[2].astype(jnp.float32)
    cot_data = arrived[3].astype(jnp.float32)
    repeated = jnp.tile(filters, (local_ch // filter_count, 1))
    filter_full = lax.all_to_all(repeated, "ctx", split_axis=0, concat_axis=1, tiled=True)
    product = key_data * value_data
    adjoint = cot_data * queries
    spec_real, spec_imag = forward_padded(jnp.concatenate([product, adjoint, filter_full], axis=0))
    prod_real, prod_imag = (spec_real[:per_device], spec_imag[:per_device])
    adj_real = spec_real[per_device : 2 * per_device]
    adj_imag = spec_imag[per_device : 2 * per_device]
    filt_real, filt_imag = (spec_real[2 * per_device :], spec_imag[2 * per_device :])
    mix_real = filt_real * prod_real - filt_imag * prod_imag
    mix_imag = filt_real * prod_imag + filt_imag * prod_real
    back_real = filt_real * adj_real + filt_imag * adj_imag
    back_imag = filt_real * adj_imag - filt_imag * adj_real
    corr_real = adj_real * prod_real + adj_imag * prod_imag
    corr_imag = adj_imag * prod_real - adj_real * prod_imag
    joint_real = jnp.concatenate([mix_real - back_imag, corr_real], axis=0)
    joint_imag = jnp.concatenate([mix_imag + back_real, corr_imag], axis=0)
    out_real, out_imag = inverse_half(joint_real, joint_imag)
    inv_scale = 1.0 / padded_len
    conv_out = out_real[:per_device] * inv_scale
    conv_back = out_imag[:per_device] * inv_scale
    filter_rows = out_real[per_device:] * inv_scale
    returned = lax.all_to_all(
        jnp.stack([conv_out, conv_back], axis=0), "ctx", split_axis=2, concat_axis=1, tiled=True
    )
    query_grad = (cotangent.astype(jnp.float32) * returned[0]).astype(jnp.bfloat16)
    key_grad = (returned[1] * value_stream.astype(jnp.float32)).astype(jnp.bfloat16)
    value_grad = (returned[1] * key_stream.astype(jnp.float32)).astype(jnp.bfloat16)
    grad_scale = 1.0 / math.sqrt(GROUP * seq_len)
    base_rows = lax.all_to_all(filter_rows, "ctx", split_axis=1, concat_axis=0, tiled=True)
    folded = base_rows.reshape(local_ch // filter_count, filter_count, length).sum(axis=0)
    filter_grad = lax.psum(folded, "chan") * grad_scale
    return (query_grad, key_grad, value_grad, filter_grad)


def solution(mesh):
    in_specs = (
        P("chan", ("groups", "ctx")),
        P("chan", ("groups", "ctx")),
        P("chan", ("groups", "ctx")),
        P("chan", ("groups", "ctx")),
        P(None, "ctx"),
    )
    out_specs = (
        P("chan", ("groups", "ctx")),
        P("chan", ("groups", "ctx")),
        P("chan", ("groups", "ctx")),
        P(None, ("groups", "ctx")),
    )
    chosen = body
    if mesh.shape["ctx"] == 4:
        chosen = blocked_body
    return jax.shard_map(chosen, mesh=mesh, in_specs=in_specs, out_specs=out_specs, check_vma=False)
```

profile of v0, /device:TPU:1, one launch (start us, length us, event | category | flops | bytes accessed | tf_op | source)
XLA Modules:
  0.0 149.2 jit_solution(4375189424221383467)
XLA Ops:
  7.2 0.0 reduce-scatter.2.cloned.1.call-start
  7.2 0.0 copy-start
  7.2 1.0 copy-done
  8.3 0.0 copy-start.1
  8.3 1.0 copy-done.1
  9.3 0.0 copy-start.2
  9.3 1.0 copy-done.2
  10.3 0.0 copy-start.3
  10.3 1.0 copy-done.3
  11.4 0.0 copy-start.4
  11.4 0.9 copy-done.4
  12.3 1.1 copy-done.5
  13.5 1.1 copy-done.6
  14.6 65.7 %shard_map.102 = (bf16[1024,256]{1,0:T(8,128)(2,1)S(1)}, bf16[1024,256]{1,0:T(8,128)(2,1)S(1)}, bf16[1024,256]{1,0:T(8,128)(2,1)S(1)}, f32[4,256,256]{2,1,0:T(8,128)}) custom-call(bf16[1024,256]{1,0:T(8,128)(2,1)S(1)} %copy-done, bf16[1024,256]{1,0:T(8,128)(2,1)S(1)} %copy-done.1, bf16[1024,256]{1,0:T(8,128)(2,1)S(1)} %copy-done.2, ...), custom_call_target="tpu_custom_call" | custom-call | flops 8000000000 | bytes 8000000 | tf_op jit(solution)/shard_map/pallas_call | solution.py:360
  80.3 0.0 reduce-scatter.2.cloned.1.call-update
  80.4 0.0 all-reduce.2.cloned.1.call-start
  80.4 26.8 %reduce-scatter.2.cloned.1.call-done = f32[1,256,256]{2,1,0:T(8,128)} async-done(((f32[4,256,256]{2,1,0:T(8,128)}), f32[1,256,256]{2,1,0:T(8,128)}) %reduce-scatter.2.cloned.1.call-update) | async-done | bytes 262160 | tf_op jit(solution)/shard_map/reduce_scatter | solution.py:395
  107.2 0.0 all-reduce.2.cloned.1.call-update
  107.2 31.7 %all-reduce.2.cloned.1.call-done = f32[256,256]{1,0:T(8,128)} async-done(((f32[256,256]{1,0:T(8,128)}), f32[256,256]{1,0:T(8,128)}) %all-reduce.2.cloned.1.call-update) | async-done | bytes 262160 | tf_op jit(solution)/shard_map/psum | solution.py:396
  139.0 0.8 copy.15
  139.8 0.8 copy.16
  140.6 0.8 copy.17
  141.4 0.3 copy-done.7
  141.7 0.7 copy.18
  (3 shorter events, 0.0 us)
Async XLA Ops:
  7.2 100.0 %reduce-scatter.2.cloned.1.call-start = ((), (), s32[]{:S(2)}) async-start(), calls=%async_computation.1 | async-start | bytes 1310720 | tf_op jit(solution)/shard_map/reduce_scatter | solution.py:395
  7.2 1.0 copy-start
  8.3 1.0 copy-start.1
  9.3 1.0 copy-start.2
  10.3 1.0 copy-start.3
  11.4 0.9 copy-start.4
  12.3 1.1 copy-start.5
  13.5 1.1 copy-start.6
  80.4 58.6 %all-reduce.2.cloned.1.call-start = ((), (), s32[]{:S(2)}) async-start(), calls=%async_computation.2 | async-start | bytes 524288 | tf_op jit(solution)/shard_map/psum | solution.py:396
  140.6 1.1 copy-start.7
Sparse Core Ops, SparseCore 0:
  80.5 26.6 reduce-scatter.1
  109.7 29.2 all-reduce.1
where the time goes:
time: 152 us; the launch traced here: 149 us
  Pallas kernels  65.7 us (43%)
  waiting for transfers between devices  58.6 us (39%)
  between operations  14.1 us (9%)
  local copies, waits for them, and re-layouts  10.8 us (7%)
    pallas_call x1, Pallas kernels, blocked_body(): pl.pallas_call(functools.partial(ctx_kernel, nchan), out_shape=(stream, s...  65.7 us
    psum x1, waiting for transfers between devices, blocked_body(): filter_grad = lax.psum(summed.reshape(fcount, block), 'chan')  31.7 us
    reduce_scatter x1, waiting for transfers between devices, blocked_body(): summed = lax.psum_scatter(terms, 'ctx', scatter_dimension=0, tiled=True)  26.8 us
    unnamed x20, local copies, waits for them, and re-layouts  10.8 us
  transfers between devices with their start and end apart: 2, of which 2 were waited for; matrix products, arithmetic and copies ran while one was open for 0% of the time, Pallas kernels for 0%

commit v1 on v0

--- a/solution.py
+++ b/solution.py
@@ -36,6 +36,17 @@
 
 def ctx_kernel(
     nchan,
+    q_far,
+    k_far,
+    v_far,
+    c_far,
+    filt_far,
+    ahead_far,
+    back_far,
+    qg_ref,
+    kg_ref,
+    vg_ref,
+    fg_ref,
     q_ref,
     k_ref,
     v_ref,
@@ -43,10 +54,11 @@
     filt_ref,
     ahead_ref,
     back_ref,
-    qg_ref,
-    kg_ref,
-    vg_ref,
-    fg_ref,
+    fg_loc,
+    fg_stage,
+    fg_part,
+    fg_ctx,
+    fg_fin,
     pair_p,
     pair_a,
     landed,
@@ -65,6 +77,13 @@
     spread_recv,
     agg_send,
     agg_recv,
+    near_sem,
+    sum_send,
+    sum_recv,
+    own_send,
+    own_recv,
+    fin_send,
+    fin_recv,
 ):
     local_ch, block = q_ref.shape
     fcount = filt_ref.shape[0]
@@ -74,6 +93,22 @@
     mine = lax.axis_index("chan")
     f32, bf16 = jnp.float32, jnp.bfloat16
 
+    near = [
+        pltpu.make_async_copy(src, dst, near_sem.at[at])
+        for at, (src, dst) in enumerate(
+            (
+                (filt_far, filt_ref),
+                (k_far, k_ref),
+                (v_far, v_ref),
+                (c_far, c_ref),
+                (q_far, q_ref),
+                (ahead_far, ahead_ref),
+                (back_far, back_ref),
+            )
+        )
+    ]
+    for copy in near:
+        copy.start()
     barrier = pltpu.get_barrier_semaphore()
     for step in range(1, 4):
         pl.semaphore_signal(
@@ -90,12 +125,14 @@
         dest[rows, 0:block] = high
         dest[rows, block : 2 * block] = (val - high.astype(f32)).astype(bf16)
 
-    @pl.loop(0, local_ch // 64)
-    def _(i):
-        rows = pl.ds(pl.multiple_of(i * 64, 64), 64)
-        split_into(pair_p, rows, k_ref[rows, :], v_ref[rows, :])
-        split_into(pair_a, rows, c_ref[rows, :], q_ref[rows, :])
-
+    def make_pairs(dest, left, right, chunk):
+        @pl.loop(0, fcount // 64)
+        def _(i):
+            rows = pl.ds(pl.multiple_of(chunk * fcount + i * 64, 64), 64)
+            split_into(dest, rows, left[rows, :], right[rows, :])
+
+    for copy in near[:5]:
+        copy.wait()
     pl.semaphore_wait(barrier, 3 + nchan - 1)
 
     def move(source, chunk, slot, target):
@@ -139,6 +176,39 @@
             send_sem=agg_send.at[chunk],
             recv_sem=agg_recv.at[chunk],
             device_id={"ctx": target},
+            device_id_type=MESH,
+        )
+
+    def sum_move(blocks, step):
+        peer = lax.rem(mine + step, nchan)
+        rows = pl.ds(pl.multiple_of(peer * quarter, quarter), quarter)
+        return pltpu.make_async_remote_copy(
+            src_ref=fg_loc.at[blocks, rows, :],
+            dst_ref=fg_stage.at[step, blocks, :, :],
+            send_sem=sum_send.at[step],
+            recv_sem=sum_recv.at[step],
+            device_id={"chan": peer},
+            device_id_type=MESH,
+        )
+
+    def own_move(target, source):
+        return pltpu.make_async_remote_copy(
+            src_ref=fg_part.at[target],
+            dst_ref=fg_ctx.at[source],
+            send_sem=own_send.at[target],
+            recv_sem=own_recv.at[source],
+            device_id={"ctx": target},
+            device_id_type=MESH,
+        )
+
+    def fin_move(step):
+        rows = pl.ds(pl.multiple_of(mine * quarter, quarter), quarter)
+        return pltpu.make_async_remote_copy(
+            src_ref=fg_fin.at[rows, :],
+            dst_ref=fg_fin.at[rows, :],
+            send_sem=fin_send.at[step],
+            recv_sem=fin_recv.at[step],
+            device_id={"chan": lax.rem(mine + step, nchan)},
             device_id_type=MESH,
         )
 
@@ -180,7 +250,10 @@
             copy = filt_move(j, target)
             copy.start()
             sends.append(copy)
+        from_p, from_a = (pair_p, k_ref, v_ref), (pair_a, c_ref, q_ref)
+        first, second = (from_p, from_a) if lower else (from_a, from_p)
         for chunk in range(chunks):
+            make_pairs(*first, chunk)
             if inner:
                 moves = [move(own_u, chunk, 1, 3 - j)]
             else:
@@ -191,6 +264,10 @@
             for copy in moves:
                 copy.start()
                 sends.append(copy)
+        for chunk in range(chunks):
+            make_pairs(*second, chunk)
+        for copy in near[5:]:
+            copy.wait()
         for owner in needs:
             filt_move(owner, j).wait_recv()
             for step in range(1, nchan):
@@ -312,10 +389,7 @@
                 vg_ref[crow, :] = (back * k_ref[crow, :].astype(f32)).astype(bf16)
 
         scale = 1.0 / math.sqrt(GROUP * block * 4)
-        for b in range(4):
-            if b not in used:
-                fg_ref[b, :, :] = jnp.zeros((fcount, block), f32)
-                continue
+        for b in used:
 
             @pl.loop(0, fcount // ROWS)
             def _(i):
@@ -327,7 +401,25 @@
                     im = im - sign * corr[b + 1, rows, 0:block]
                 put_prep(0, rows, re, im)
 
-            fg_ref[b, :, :] = inverse_of(0) * scale
+            fg_loc[b, :, :] = inverse_of(0) * scale
+        blocks = pl.ds(0, len(used))
+        for step in range(1, nchan):
+            copy = sum_move(blocks, step)
+            copy.start()
+            sends.append(copy)
+        my_rows = pl.ds(pl.multiple_of(mine * quarter, quarter), quarter)
+        for step in range(1, nchan):
+            sum_move(blocks, step).wait_recv()
+        for b in used:
+            total = fg_loc[b, my_rows, :]
+            for step in range(1, nchan):
+                total = total + fg_stage[step, b, :, :]
+            fg_part[b, :, :] = total
+        for b in used:
+            if b != j:
+                copy = own_move(b, j)
+                copy.start()
+                sends.append(copy)
 
         if not inner:
             for chunk in range(chunks):
@@ -339,6 +431,19 @@
                 else:
                     kg_ref[crow, :] = (total * v_ref[crow, :].astype(f32)).astype(bf16)
                     vg_ref[crow, :] = (total * k_ref[crow, :].astype(f32)).astype(bf16)
+        total = fg_part[j, :, :] if j in used else None
+        for src in {0: (1, 2, 3), 1: (2,), 2: (1,), 3: (1, 2)}[j]:
+            own_move(j, src).wait_recv()
+            term = fg_ctx[src, :, :]
+            total = term if total is None else total + term
+        fg_fin[my_rows, :] = total
+        for step in range(1, nchan):
+            copy = fin_move(step)
+            copy.start()
+            sends.append(copy)
+        for step in range(1, nchan):
+            fin_move(step).wait_recv()
+        fg_ref[...] = fg_fin[...]
         for copy in sends:
             copy.wait_send()
 
@@ -357,17 +462,30 @@
     vmem = pl.BlockSpec(memory_space=pltpu.VMEM)
     stream = jax.ShapeDtypeStruct((local_ch, block), jnp.bfloat16)
     dma = pltpu.SemaphoreType.DMA
-    query_grad, key_grad, value_grad, terms = pl.pallas_call(
+    quarter = fcount // nchan
+    return pl.pallas_call(
         functools.partial(ctx_kernel, nchan),
         out_shape=(
             stream,
             stream,
             stream,
-            jax.ShapeDtypeStruct((4, fcount, block), jnp.float32),
+            jax.ShapeDtypeStruct((fcount, block), jnp.float32),
         ),
-        in_specs=[vmem] * 7,
+        in_specs=[pl.BlockSpec(memory_space=pltpu.HBM)] * 7,
         out_specs=(vmem,) * 4,
         scratch_shapes=[
+            pltpu.VMEM((local_ch, block), jnp.bfloat16),
+            pltpu.VMEM((local_ch, block), jnp.bfloat16),
+            pltpu.VMEM((local_ch, block), jnp.bfloat16),
+            pltpu.VMEM((local_ch, block), jnp.bfloat16),
+            pltpu.VMEM((fcount, block), jnp.float32),
+            pltpu.VMEM((3 * block, 2 * block), jnp.bfloat16),
+            pltpu.VMEM((6 * block, block), jnp.bfloat16),
+            pltpu.VMEM((4, fcount, block), jnp.float32),
+            pltpu.VMEM((nchan, 4, quarter, block), jnp.float32),
+            pltpu.VMEM((4, quarter, block), jnp.float32),
+            pltpu.VMEM((4, quarter, block), jnp.float32),
+            pltpu.VMEM((fcount, block), jnp.float32),
             pltpu.VMEM((local_ch, 2 * block), jnp.bfloat16),
             pltpu.VMEM((local_ch, 2 * block), jnp.bfloat16),
             pltpu.VMEM((3, local_ch, 2 * block), jnp.bfloat16),
@@ -386,15 +504,19 @@
             dma((4, nchan)),
             dma((chunks,)),
             dma((chunks,)),
+            dma((7,)),
+            dma((nchan,)),
+            dma((nchan,)),
+            dma((4,)),
+            dma((4,)),
+            dma((nchan,)),
+            dma((nchan,)),
         ],
         compiler_params=pltpu.CompilerParams(
-            collective_id=0, has_side_effects=True, vmem_limit_bytes=48 * 1024 * 1024
+            collective_id=0, has_side_effects=True, vmem_limit_bytes=60 * 1024 * 1024
         ),
         cost_estimate=pl.CostEstimate(flops=8 * 10**9, bytes_accessed=8 * 10**6, transcendentals=0),
     )(query_stream, key_stream, value_stream, cotangent, filters, ahead, back)
-    summed = lax.psum_scatter(terms, "ctx", scatter_dimension=0, tiled=True)
-    filter_grad = lax.psum(summed.reshape(fcount, block), "chan")
-    return (query_grad, key_grad, value_grad, filter_grad)
 
 
 highest_mode = lax.Precision.HIGHEST

time: 152 us -> 88.9 us (0.58); the launches traced: 149 us -> 88.7 us
  waiting for transfers between devices: 58.6 us -> 0 us
  Pallas kernels: 65.7 us -> 83.1 us
  between operations: 14.1 us -> 0.65 us
  local copies, waits for them, and re-layouts: 10.8 us -> 4.95 us
    psum x1 -> x0, waiting for transfers between devices: 31.7 us -> none  [blocked_body(): filter_grad = lax.psum(summed.reshape(fcount, block), 'chan')]
    reduce_scatter x1 -> x0, waiting for transfers between devices: 26.8 us -> none  [blocked_body(): summed = lax.psum_scatter(terms, 'ctx', scatter_dimension=0, tiled=True)]
    pallas_call x1, Pallas kernels: 65.7 us -> 83.1 us  [blocked_body(): pl.pallas_call(functools.partial(ctx_kernel, nchan), out_shape=(stream, s...]
    unnamed x20 -> x10, local copies, waits for them, and re-layouts: 10.8 us -> 4.95 us
  transfers between devices with their start and end apart: 2 -> 0, of which waited for: 2 -> 0; matrix products, arithmetic and copies ran while one was open for 0% -> 0% of each run, Pallas kernels for 0% -> 0%
where the time goes in v1:
time: 88.9 us; the launch traced here: 88.7 us
  Pallas kernels  83.1 us (93%)
  local copies, waits for them, and re-layouts  4.95 us (6%)
    pallas_call x1, Pallas kernels, blocked_body(): pl.pallas_call(functools.partial(ctx_kernel, nchan), out_shape=(stream, s...  83.1 us
    unnamed x10, local copies, waits for them, and re-layouts  4.95 us

profile of v1, /device:TPU:1, one launch (start us, length us, event | category | flops | bytes accessed | tf_op | source)
XLA Modules:
  0.0 88.7 jit_solution(6285647526710181038)
XLA Ops:
  0.6 83.1 %shard_map.102 = (bf16[1024,256]{1,0:T(8,128)(2,1)}, bf16[1024,256]{1,0:T(8,128)(2,1)}, bf16[1024,256]{1,0:T(8,128)(2,1)}, f32[256,256]{1,0:T(8,128)}) custom-call(bf16[1024,256]{1,0:T(8,128)(2,1)} %q_far.1, bf16[1024,256]{1,0:T(8,128)(2,1)} %k_far.1, bf16[1024,256]{1,0:T(8,128)(2,1)} %v_far.1, bf16[1024,256]{1,0:T(8,128)(2,1)} %c_far.1, ...), custom_call_target="tpu_custom_call" | custom-call | flops 8000000000 | bytes 8000000 | tf_op jit(solution)/shard_map/pallas_call | solution.py:466
  83.7 0.0 copy-start.1
  83.7 1.9 %copy.15 = bf16[1024,256]{1,0:T(8,128)(2,1)} copy(bf16[1024,256]{1,0:T(8,128)(2,1)} %get-tuple-element.8) | data formatting | bytes 1048576
  85.7 0.0 copy-done.1
  85.7 0.0 copy-start
  85.7 0.8 copy.16
  86.5 0.4 copy-done
  86.9 0.0 copy-start.2
  86.9 0.8 copy.17
  87.7 0.3 copy-done.2
  88.0 0.7 copy.18
Async XLA Ops:
  83.7 1.9 %copy-start.1 = (bf16[1024,256]{1,0:T(8,128)(2,1)S(1)}, bf16[1024,256]{1,0:T(8,128)(2,1)}, u32[]{:S(2)}) copy-start(bf16[1024,256]{1,0:T(8,128)(2,1)} %get-tuple-element.9) | copy-start | bytes 1572868
  85.7 1.2 %copy-start = (bf16[1024,256]{1,0:T(8,128)(2,1)S(1)}, bf16[1024,256]{1,0:T(8,128)(2,1)}, u32[]{:S(2)}) copy-start(bf16[1024,256]{1,0:T(8,128)(2,1)} %get-tuple-element.10) | copy-start | bytes 1572868
  86.9 1.1 %copy-start.2 = (f32[256,256]{1,0:T(8,128)S(1)}, f32[256,256]{1,0:T(8,128)}, u32[]{:S(2)}) copy-start(f32[256,256]{1,0:T(8,128)} %get-tuple-element.11) | copy-start | bytes 786436

commit v2 on v1

--- a/solution.py
+++ b/solution.py
@@ -85,10 +85,10 @@
     fin_send,
     fin_recv,
 ):
-    local_ch, block = q_ref.shape
-    fcount = filt_ref.shape[0]
-    chunks = local_ch // fcount
+    copies, fcount, block = q_ref.shape
+    chunks = nchan
     quarter = fcount // nchan
+    crows = copies * quarter
     me = lax.axis_index("ctx")
     mine = lax.axis_index("chan")
     f32, bf16 = jnp.float32, jnp.bfloat16
@@ -119,27 +119,33 @@
             barrier, inc=1, device_id={"chan": lax.rem(mine + step, nchan)}, device_id_type=MESH
         )
 
+    def first_row(chunk):
+        return pl.multiple_of(lax.rem(mine + 1 + chunk, nchan) * quarter, quarter)
+
+    def rows_of(chunk):
+        return pl.ds(first_row(chunk), quarter)
+
     def split_into(dest, rows, left, right):
         val = left.astype(f32) * right.astype(f32)
         high = val.astype(bf16)
-        dest[rows, 0:block] = high
-        dest[rows, block : 2 * block] = (val - high.astype(f32)).astype(bf16)
+        dest[:, rows, 0:block] = high
+        dest[:, rows, block : 2 * block] = (val - high.astype(f32)).astype(bf16)
 
     def make_pairs(dest, left, right, chunk):
-        @pl.loop(0, fcount // 64)
+        @pl.loop(0, quarter // ROWS)
         def _(i):
-            rows = pl.ds(pl.multiple_of(chunk * fcount + i * 64, 64), 64)
-            split_into(dest, rows, left[rows, :], right[rows, :])
+            rows = pl.ds(pl.multiple_of(first_row(chunk) + i * ROWS, ROWS), ROWS)
+            split_into(dest, rows, left[:, rows, :], right[:, rows, :])
 
     for copy in near[:5]:
         copy.wait()
     pl.semaphore_wait(barrier, 3 + nchan - 1)
 
     def move(source, chunk, slot, target):
-        rows = pl.ds(chunk * fcount, fcount)
+        rows = rows_of(chunk)
         return pltpu.make_async_remote_copy(
-            src_ref=source.at[rows, :],
-            dst_ref=landed.at[slot, rows, :],
+            src_ref=source.at[:, rows, :],
+            dst_ref=landed.at[slot, :, rows, :],
             send_sem=send_sem.at[slot, chunk],
             recv_sem=recv_sem.at[slot, chunk],
             device_id={"ctx": target},
@@ -169,10 +175,10 @@
         )
 
     def agg_move(chunk, target):
-        rows = pl.ds(chunk * fcount, fcount)
+        rows = rows_of(chunk)
         return pltpu.make_async_remote_copy(
-            src_ref=agg_out.at[rows, :],
-            dst_ref=agg_in.at[rows, :],
+            src_ref=agg_out.at[:, rows, :],
+            dst_ref=agg_in.at[:, rows, :],
             send_sem=agg_send.at[chunk],
             recv_sem=agg_recv.at[chunk],
             device_id={"ctx": target},
@@ -181,9 +187,8 @@
 
     def sum_move(blocks, step):
         peer = lax.rem(mine + step, nchan)
-        rows = pl.ds(pl.multiple_of(peer * quarter, quarter), quarter)
         return pltpu.make_async_remote_copy(
-            src_ref=fg_loc.at[blocks, rows, :],
+            src_ref=fg_loc.at[step, blocks, :, :],
             dst_ref=fg_stage.at[step, blocks, :, :],
             send_sem=sum_send.at[step],
             recv_sem=sum_recv.at[step],
@@ -219,13 +224,14 @@
         )
 
     def inverse_of(which):
-        return jnp.dot(
+        val = jnp.dot(
             prep[which, :, :], back_ref[0 : 4 * block, :], preferred_element_type=f32
         ) + jnp.dot(
             prep[which, :, 0 : 2 * block],
             back_ref[4 * block : 6 * block, :],
             preferred_element_type=f32,
         )
+        return val.reshape(copies, quarter, block)
 
     def put_prep(which, rows, re, im):
         for place, val in ((0, re), (block, im)):
@@ -296,7 +302,6 @@
                     im = im + sign * spec[d - 1, rows, 0:block]
                 gains[d, rows, 0:block] = re
                 gains[d, rows, block : 2 * block] = im
-                corr[d, rows, :] = jnp.zeros((ROWS, 2 * block), f32)
 
         if inner:
             held_p = {1: (0, 1), 2: (0, 1, 2)}[j]
@@ -317,25 +322,33 @@
             3: ((3, 3),),
         }[j]
 
+        scale = 1.0 / math.sqrt(GROUP * block * 4)
+        blocks = pl.ds(0, len(used))
         for chunk in range(chunks):
-            crow = pl.ds(chunk * fcount, fcount)
+            crow = rows_of(chunk)
+            corr[...] = jnp.zeros(corr.shape, f32)
             for name, place in places.items():
                 if name in slots:
                     move(own_u, chunk, slots[name], j).wait_recv()
-                    spec[place, :, :] = ahead(landed[slots[name], crow, :])
+                    spec[place, :, :] = ahead(landed[slots[name], :, crow, :].reshape(crows, 2 * block))
                 else:
-                    spec[place, :, :] = ahead((pair_p if name[0] == "p" else pair_a)[crow, :])
-
-            @pl.loop(0, fcount // ROWS)
+                    spec[place, :, :] = ahead(
+                        (pair_p if name[0] == "p" else pair_a)[:, crow, :].reshape(crows, 2 * block)
+                    )
+
+            @pl.loop(0, crows // ROWS)
             def _(i):
                 rows = pl.ds(pl.multiple_of(i * ROWS, ROWS), ROWS)
+                place_in = lax.rem(i, quarter // ROWS) * ROWS
+                frows = pl.ds(pl.multiple_of(first_row(chunk) + place_in, ROWS), ROWS)
+                drows = pl.ds(pl.multiple_of(place_in, ROWS), ROWS)
 
                 def load(name):
                     at = places[name]
                     return spec[at, rows, 0:block], spec[at, rows, block : 2 * block]
 
                 def gain(d):
-                    return gains[d, rows, 0:block], gains[d, rows, block : 2 * block]
+                    return gains[d, frows, 0:block], gains[d, frows, block : 2 * block]
 
                 def mixed_to(target):
                     re = im = None
@@ -369,49 +382,51 @@
                     pr, pi = load(("p", src))
                     ar, ai = load(("a", dst))
                     d = dst - src
-                    corr[d, rows, 0:block] += ar * pr + ai * pi
-                    corr[d, rows, block : 2 * block] += ai * pr - ar * pi
+                    corr[d, drows, 0:block] += ar * pr + ai * pi
+                    corr[d, drows, block : 2 * block] += ai * pr - ar * pi
 
             if inner:
-                agg_out[crow, :] = inverse_of(2)
+                agg_out[:, crow, :] = inverse_of(2)
                 copy = agg_move(chunk, 0 if lower else 3)
                 copy.start()
                 sends.append(copy)
             if j == 3:
-                agg_out[crow, :] = inverse_of(0)
+                agg_out[:, crow, :] = inverse_of(0)
             else:
-                qg_ref[crow, :] = (c_ref[crow, :].astype(f32) * inverse_of(0)).astype(bf16)
+                qg_ref[:, crow, :] = (c_ref[:, crow, :].astype(f32) * inverse_of(0)).astype(bf16)
             if j == 0:
-                agg_out[crow, :] = inverse_of(1)
+                agg_out[:, crow, :] = inverse_of(1)
             else:
                 back = inverse_of(1)
-                kg_ref[crow, :] = (back * v_ref[crow, :].astype(f32)).astype(bf16)
-                vg_ref[crow, :] = (back * k_ref[crow, :].astype(f32)).astype(bf16)
-
-        scale = 1.0 / math.sqrt(GROUP * block * 4)
-        for b in used:
-
-            @pl.loop(0, fcount // ROWS)
-            def _(i):
-                rows = pl.ds(pl.multiple_of(i * ROWS, ROWS), ROWS)
-                re, im = corr[b, rows, 0:block], corr[b, rows, block : 2 * block]
-                if b + 1 in used:
-                    sign = sign_of()
-                    re = re + sign * corr[b + 1, rows, block : 2 * block]
-                    im = im - sign * corr[b + 1, rows, 0:block]
-                put_prep(0, rows, re, im)
-
-            fg_loc[b, :, :] = inverse_of(0) * scale
-        blocks = pl.ds(0, len(used))
-        for step in range(1, nchan):
-            copy = sum_move(blocks, step)
-            copy.start()
-            sends.append(copy)
+                kg_ref[:, crow, :] = (back * v_ref[:, crow, :].astype(f32)).astype(bf16)
+                vg_ref[:, crow, :] = (back * k_ref[:, crow, :].astype(f32)).astype(bf16)
+
+            for b in used:
+
+                @pl.loop(0, quarter // ROWS)
+                def _(i):
+                    rows = pl.ds(pl.multiple_of(i * ROWS, ROWS), ROWS)
+                    re, im = corr[b, rows, 0:block], corr[b, rows, block : 2 * block]
+                    if b + 1 in used:
+                        sign = sign_of()
+                        re = re + sign * corr[b + 1, rows, block : 2 * block]
+                        im = im - sign * corr[b + 1, rows, 0:block]
+                    put_prep(0, pl.ds(pl.multiple_of(b * quarter + i * ROWS, ROWS), ROWS), re, im)
+
+            place = chunk + 1 if chunk < chunks - 1 else 0
+            terms = inverse_of(0).reshape(crows, block) * scale
+            for b in used:
+                fg_loc[place, b, :, :] = terms[b * quarter : (b + 1) * quarter, :]
+            if place:
+                copy = sum_move(blocks, place)
+                copy.start()
+                sends.append(copy)
+
         my_rows = pl.ds(pl.multiple_of(mine * quarter, quarter), quarter)
         for step in range(1, nchan):
             sum_move(blocks, step).wait_recv()
         for b in used:
-            total = fg_loc[b, my_rows, :]
+            total = fg_loc[0, b, :, :]
             for step in range(1, nchan):
                 total = total + fg_stage[step, b, :, :]
             fg_part[b, :, :] = total
@@ -423,14 +438,14 @@
 
         if not inner:
             for chunk in range(chunks):
-                crow = pl.ds(chunk * fcount, fcount)
+                crow = rows_of(chunk)
                 agg_move(chunk, j).wait_recv()
-                total = agg_out[crow, :] + agg_in[crow, :]
+                total = agg_out[:, crow, :] + agg_in[:, crow, :]
                 if j == 3:
-                    qg_ref[crow, :] = (c_ref[crow, :].astype(f32) * total).astype(bf16)
+                    qg_ref[:, crow, :] = (c_ref[:, crow, :].astype(f32) * total).astype(bf16)
                 else:
-                    kg_ref[crow, :] = (total * v_ref[crow, :].astype(f32)).astype(bf16)
-                    vg_ref[crow, :] = (total * k_ref[crow, :].astype(f32)).astype(bf16)
+                    kg_ref[:, crow, :] = (total * v_ref[:, crow, :].astype(f32)).astype(bf16)
+                    vg_ref[:, crow, :] = (total * k_ref[:, crow, :].astype(f32)).astype(bf16)
         total = fg_part[j, :, :] if j in used else None
         for src in {0: (1, 2, 3), 1: (2,), 2: (1,), 3: (1, 2)}[j]:
             own_move(j, src).wait_recv()
@@ -455,15 +470,17 @@
     local_ch, block = query_stream.shape
     fcount = filters.shape[0]
     nchan = lax.axis_size("chan")
-    chunks = local_ch // fcount
+    copies = local_ch // fcount
+    shape = (copies, fcount, block)
     ahead, back = half_tables(block)
     ahead = jnp.asarray(ahead)
     back = jnp.asarray(back)
     vmem = pl.BlockSpec(memory_space=pltpu.VMEM)
-    stream = jax.ShapeDtypeStruct((local_ch, block), jnp.bfloat16)
+    stream = jax.ShapeDtypeStruct(shape, jnp.bfloat16)
     dma = pltpu.SemaphoreType.DMA
     quarter = fcount // nchan
-    return pl.pallas_call(
+    chunks, crows = nchan, copies * quarter
+    *grads, filter_grad = pl.pallas_call(
         functools.partial(ctx_kernel, nchan),
         out_shape=(
             stream,
@@ -474,28 +491,28 @@
         in_specs=[pl.BlockSpec(memory_space=pltpu.HBM)] * 7,
         out_specs=(vmem,) * 4,
         scratch_shapes=[
-            pltpu.VMEM((local_ch, block), jnp.bfloat16),
-            pltpu.VMEM((local_ch, block), jnp.bfloat16),
-            pltpu.VMEM((local_ch, block), jnp.bfloat16),
-            pltpu.VMEM((local_ch, block), jnp.bfloat16),
+            pltpu.VMEM(shape, jnp.bfloat16),
+            pltpu.VMEM(shape, jnp.bfloat16),
+            pltpu.VMEM(shape, jnp.bfloat16),
+            pltpu.VMEM(shape, jnp.bfloat16),
             pltpu.VMEM((fcount, block), jnp.float32),
             pltpu.VMEM((3 * block, 2 * block), jnp.bfloat16),
             pltpu.VMEM((6 * block, block), jnp.bfloat16),
-            pltpu.VMEM((4, fcount, block), jnp.float32),
+            pltpu.VMEM((nchan, 4, quarter, block), jnp.float32),
             pltpu.VMEM((nchan, 4, quarter, block), jnp.float32),
             pltpu.VMEM((4, quarter, block), jnp.float32),
             pltpu.VMEM((4, quarter, block), jnp.float32),
             pltpu.VMEM((fcount, block), jnp.float32),
-            pltpu.VMEM((local_ch, 2 * block), jnp.bfloat16),
-            pltpu.VMEM((local_ch, 2 * block), jnp.bfloat16),
-            pltpu.VMEM((3, local_ch, 2 * block), jnp.bfloat16),
+            pltpu.VMEM((copies, fcount, 2 * block), jnp.bfloat16),
+            pltpu.VMEM((copies, fcount, 2 * block), jnp.bfloat16),
+            pltpu.VMEM((3, copies, fcount, 2 * block), jnp.bfloat16),
             pltpu.VMEM((4, fcount, block), jnp.float32),
             pltpu.VMEM((4, fcount, 2 * block), jnp.float32),
-            pltpu.VMEM((5, fcount, 2 * block), jnp.float32),
-            pltpu.VMEM((3, fcount, 4 * block), jnp.bfloat16),
-            pltpu.VMEM((4, fcount, 2 * block), jnp.float32),
-            pltpu.VMEM((local_ch, block), jnp.float32),
-            pltpu.VMEM((local_ch, block), jnp.float32),
+            pltpu.VMEM((5, max(crows, fcount), 2 * block), jnp.float32),
+            pltpu.VMEM((3, crows, 4 * block), jnp.bfloat16),
+            pltpu.VMEM((4, quarter, 2 * block), jnp.float32),
+            pltpu.VMEM(shape, jnp.float32),
+            pltpu.VMEM(shape, jnp.float32),
             dma((3, chunks)),
             dma((3, chunks)),
             dma((4,)),
@@ -516,7 +533,13 @@
             collective_id=0, has_side_effects=True, vmem_limit_bytes=60 * 1024 * 1024
         ),
         cost_estimate=pl.CostEstimate(flops=8 * 10**9, bytes_accessed=8 * 10**6, transcendentals=0),
-    )(query_stream, key_stream, value_stream, cotangent, filters, ahead, back)
+    )(
+        *(x.reshape(shape) for x in (query_stream, key_stream, value_stream, cotangent)),
+        filters,
+        ahead,
+        back,
+    )
+    return (*(x.reshape(local_ch, block) for x in grads), filter_grad)
 
 
 highest_mode = lax.Precision.HIGHEST

time: 88.9 us -> 80.8 us (0.909)
  Pallas kernels: 83.1 us -> 74.9 us
    pallas_call x1, Pallas kernels: 83.1 us -> 74.9 us  [blocked_body(): pl.pallas_call(functools.partial(ctx_kernel, nchan), out_shape=(stream, s...]
where the time goes in v2:
time: 80.8 us; the launch traced here: 80.5 us
  Pallas kernels  74.9 us (93%)
  local copies, waits for them, and re-layouts  4.95 us (6%)
    pallas_call x1, Pallas kernels, blocked_body(): pl.pallas_call(functools.partial(ctx_kernel, nchan), out_shape=(stream, s...  74.9 us
    unnamed x10, local copies, waits for them, and re-layouts  4.95 us

profile of v2, /device:TPU:1, one launch (start us, length us, event | category | flops | bytes accessed | tf_op | source)
XLA Modules:
  0.0 80.5 jit_solution(16729406708998190119)
XLA Ops:
  0.6 74.9 %shard_map.102 = (bf16[4,256,256]{2,1,0:T(8,128)(2,1)}, bf16[4,256,256]{2,1,0:T(8,128)(2,1)}, bf16[4,256,256]{2,1,0:T(8,128)(2,1)}, f32[256,256]{1,0:T(8,128)}) custom-call(bf16[4,256,256]{2,1,0:T(8,128)(2,1)} %bitcast.10, bf16[4,256,256]{2,1,0:T(8,128)(2,1)} %bitcast.11, bf16[4,256,256]{2,1,0:T(8,128)(2,1)} %bitcast.12, bf16[4,256,256]{2,1,0:T(8,128)(2,1)} %bitcast.13, ...), custom_call_target="tpu_custom_call" | custom-call | flops 8000000000 | bytes 8000000 | tf_op jit(solution)/shard_map/pallas_call | solution.py:483
  75.6 0.0 copy-start.1
  75.6 1.9 %copy.15 = bf16[1024,256]{1,0:T(8,128)(2,1)} copy(bf16[1024,256]{1,0:T(8,128)(2,1)} %bitcast.9) | data formatting | bytes 1048576
  77.5 0.0 copy-done.1
  77.5 0.0 copy-start
  77.5 0.8 copy.16
  78.3 0.4 copy-done
  78.7 0.0 copy-start.2
  78.7 0.8 copy.17
  79.5 0.3 copy-done.2
  79.8 0.7 copy.18
Async XLA Ops:
  75.6 1.9 %copy-start.1 = (bf16[4,256,256]{2,1,0:T(8,128)(2,1)S(1)}, bf16[4,256,256]{2,1,0:T(8,128)(2,1)}, u32[]{:S(2)}) copy-start(bf16[4,256,256]{2,1,0:T(8,128)(2,1)} %get-tuple-element.9) | copy-start | bytes 1572868
  77.5 1.2 %copy-start = (bf16[4,256,256]{2,1,0:T(8,128)(2,1)S(1)}, bf16[4,256,256]{2,1,0:T(8,128)(2,1)}, u32[]{:S(2)}) copy-start(bf16[4,256,256]{2,1,0:T(8,128)(2,1)} %get-tuple-element.10) | copy-start | bytes 1572868
  78.7 1.1 %copy-start.2 = (f32[256,256]{1,0:T(8,128)S(1)}, f32[256,256]{1,0:T(8,128)}, u32[]{:S(2)}) copy-start(f32[256,256]{1,0:T(8,128)} %get-tuple-element.19) | copy-start | bytes 786436
